TPU v7x, 256 devices: a whole 4x4x8 slice. The times are simulated.
256 devices in a mesh: order: 32 (over z, x_hi, core), slab: 8 (over x_lo, y).
Axes of the slice: x: 4 (x_hi: 2, x_lo: 2; x = x_hi * 2 + x_lo), y: 4, z: 8, core: 2. Of those that a mesh axis runs over, the one named last changes fastest.
Arguments:
- direct: float32 [32, 2, 1024, 1024], P('order', None, 'slab'), may hold values from -6 to 6
- adjoint: float32 [32, 2, 1024, 1024], P('order', None, 'slab'), may hold values from -6 to 6
- sound: float32 [1024, 1024], P('slab'), may hold values from 0.5 to 4
- transverse: float32 [1024, 1024], replicated, may hold values from -0.1875 to 0.1875
- burner_temp: float32 [32], replicated, may hold values from -4 to 4
- burner_gain: float32 [32], replicated, may hold values from -4 to 4
- flame_cells: int32 [4096], replicated, may hold values from 0 to 1048575
- flame_weight: float32 [4096], replicated, may hold values from 0.5 to 4
- offsets: int32 [4], replicated, may hold values from 1 to 31
Outputs:
- image: float32 [32, 2, 1024, 1024], P('order', None, 'slab')
- coupling: float32 [32, 2, 4], P('order')
All inputs are finite; a program needn't handle non-finite values.
Results may differ from a plain program's by a relative error of at most 0.0003.
Values sent between devices are 32-bit elements; how exact they have to be, the bound alone decides.
A program may use at most 128 MiB of HBM per device.

v0:
```python
import math

import jax
import jax.numpy as jnp
from jax import lax
from jax.sharding import PartitionSpec as P


def with_halo(cells, sides, width):
    for axis, dim in sides:
        count = lax.axis_size(axis)
        ends = count - 1
        head = lax.slice_in_dim(cells, 0, width, axis=dim)
        tail = lax.slice_in_dim(cells, cells.shape[dim] - width, cells.shape[dim], axis=dim)
        cells = jnp.concatenate(
            [
                lax.ppermute(tail, axis, [(i, (i + 1) % count) for i in range(ends)]),
                cells,
                lax.ppermute(head, axis, [((i + 1) % count, i) for i in range(ends)]),
            ],
            axis=dim,
        )
    return cells


def passed_along(block, axis, distance):
    devices = range(lax.axis_size(axis))
    route = [((i - distance) % len(devices), i) for i in devices]
    return lax.ppermute(block, axis, route)


def apply_padded(padded, sound_padded, angle_now, transverse):
    center = padded[:, 1:-1]
    middle = sound_padded[1:-1]
    axial = 0.5 * (middle + sound_padded[2:]) * (center - padded[:, 2:]) + 0.5 * (
        middle + sound_padded[:-2]
    ) * (center - padded[:, :-2])
    across = jnp.einsum("cxz,zw->cxw", center, transverse, precision=lax.Precision.HIGHEST)
    seam_weight = 0.5 * (middle[:, -1] + middle[:, 0])
    cos_turn = jnp.cos(angle_now)
    sin_turn = jnp.sin(angle_now)
    first_re = center[0, :, 0]
    first_im = center[1, :, 0]
    last_re = center[0, :, -1]
    last_im = center[1, :, -1]
    ahead_re = cos_turn * first_re - sin_turn * first_im
    ahead_im = sin_turn * first_re + cos_turn * first_im
    behind_re = cos_turn * last_re + sin_turn * last_im
    behind_im = cos_turn * last_im - sin_turn * last_re
    last_add = jnp.stack([seam_weight * (last_re - ahead_re), seam_weight * (last_im - ahead_im)])
    first_add = jnp.stack(
        [seam_weight * (first_re - behind_re), seam_weight * (first_im - behind_im)]
    )
    result = axial + across
    result = result.at[:, :, -1].add(last_add)
    result = result.at[:, :, 0].add(first_add)
    return result


def fourier_pair(values, offsets, orders):
    burner = jnp.arange(orders, dtype=jnp.int32)
    turns = offsets[:, None] * burner[None, :] % orders
    angles = 2.0 * math.pi / orders * turns.astype(values.dtype)
    real_part = jnp.sum(values[None, :] * jnp.cos(angles), axis=1) / orders
    imag_part = -jnp.sum(values[None, :] * jnp.sin(angles), axis=1) / orders
    return (real_part, imag_part)


def make_term(helm, field, flame_field, temp_re, temp_im, gain_re, gain_im):
    term_re = (
        temp_re * helm[0]
        - temp_im * helm[1]
        + flame_field * (gain_re * field[0] - gain_im * field[1])
    )
    term_im = (
        temp_re * helm[1]
        + temp_im * helm[0]
        + flame_field * (gain_re * field[1] + gain_im * field[0])
    )
    return jnp.stack([term_re, term_im])


def local(
    direct, adjoint, sound, transverse, burner_temp, burner_gain, flame_cells, flame_weight, offsets
):
    orders = lax.axis_size("order")
    order_now = lax.axis_index("order")
    slab_now = lax.axis_index("slab")
    layers = direct.shape[2]
    width = direct.shape[3]
    own_field = direct[0]
    own_adjoint = adjoint[0]
    local_ids = flame_cells - slab_now * (layers * width)
    inside = (local_ids >= 0) & (local_ids < layers * width)
    placed = jnp.where(inside, flame_weight, 0.0)
    flame_flat = (
        jnp.zeros((layers * width,), jnp.float32).at[jnp.where(inside, local_ids, 0)].add(placed)
    )
    flame_field = flame_flat.reshape(layers, width)
    temp_re, temp_im = fourier_pair(burner_temp, offsets, orders)
    gain_re, gain_im = fourier_pair(burner_gain, offsets, orders)
    sound_padded = with_halo(sound, (("slab", 0),), 1)
    own_padded = with_halo(own_field, (("slab", 1),), 1)
    angle_own = 2.0 * math.pi / orders * order_now.astype(jnp.float32)
    own_helm = apply_padded(own_padded, sound_padded, angle_own, transverse)
    sources = (order_now - offsets) % orders
    bit_count = orders.bit_length() - 1
    count_offs = offsets.shape[0]
    moving = jnp.stack([own_field for which in range(count_offs)])
    for bit_index in range(bit_count):
        arrived = passed_along(moving, "order", 1 << bit_index)
        take_step = offsets >> bit_index & 1 == 1
        moving = jnp.where(take_step[:, None, None, None], arrived, moving)
    moved_padded = with_halo(moving, (("slab", 2),), 1)
    terms = []
    for which in range(count_offs):
        angle_src = 2.0 * math.pi / orders * sources[which].astype(jnp.float32)
        helm = apply_padded(moved_padded[which], sound_padded, angle_src, transverse)
        terms.append(
            make_term(
                helm,
                moving[which],
                flame_field,
                temp_re[which],
                temp_im[which],
                gain_re[which],
                gain_im[which],
            )
        )
    total = own_helm
    sums_re = []
    sums_im = []
    for which in range(count_offs):
        term = terms[which]
        total = total + term
        sums_re.append(jnp.sum(own_adjoint[0] * term[0] + own_adjoint[1] * term[1]))
        sums_im.append(jnp.sum(own_adjoint[0] * term[1] - own_adjoint[1] * term[0]))
    partial_sums = jnp.stack([jnp.stack(sums_re), jnp.stack(sums_im)])
    image_out = total[None]
    whole_sums = lax.psum(partial_sums, "slab")
    scale = 1.0 / math.sqrt(layers * lax.axis_size("slab") * width)
    return (image_out, (whole_sums * scale)[None])


def solution(mesh):
    in_specs = (
        P("order", None, "slab", None),
        P("order", None, "slab", None),
        P("slab", None),
        P(),
        P(),
        P(),
        P(),
        P(),
        P(),
    )
    out_specs = (P("order", None, "slab", None), P("order", None, None))
    return jax.shard_map(local, mesh=mesh, in_specs=in_specs, out_specs=out_specs, check_vma=False)
```

profile of v0, /device:TPU:98, one launch (start us, length us, event | category | flops | bytes accessed | tf_op | source)
XLA Modules:
  0.0 822.5 jit_solution(16515280979996378761)
XLA Ops:
  0.6 1.9 stack.114
  2.7 50.3 %collective-permute-done.4 = f32[4,2,128,1024]{3,2,1,0:T(8,128)S(1)} collective-permute-done((f32[4,2,128,1024]{3,2,1,0:T(8,128)S(1)}, f32[4,2,128,1024]{3,2,1,0:T(8,128)S(1)}, u32[]{:S(2)}, u32[]{:S(2)}) %collective-permute-start.4) | collective-permute-done | bytes 4194336 | tf_op jit(solution)/shard_map/ppermute | solution.py:29
  53.0 0.9 broadcast_select_fusion
  53.9 1.3 collective-permute-start.5
  55.3 91.0 %collective-permute-done.5 = f32[4,2,128,1024]{3,2,1,0:T(8,128)S(1)} collective-permute-done((f32[4,2,128,1024]{3,2,1,0:T(8,128)S(1)}, f32[4,2,128,1024]{3,2,1,0:T(8,128)S(1)}, u32[]{:S(2)}, u32[]{:S(2)}) %collective-permute-start.5) | collective-permute-done | bytes 4194336 | tf_op jit(solution)/shard_map/ppermute | solution.py:29
  146.3 1.5 broadcast_select_fusion.1
  147.8 4.4 collective-permute-start.6
  152.2 86.5 %collective-permute-done.6 = f32[4,2,128,1024]{3,2,1,0:T(8,128)S(1)} collective-permute-done((f32[4,2,128,1024]{3,2,1,0:T(8,128)S(1)}, f32[4,2,128,1024]{3,2,1,0:T(8,128)S(1)}, u32[]{:S(2)}, u32[]{:S(2)}) %collective-permute-start.6) | collective-permute-done | bytes 4194336 | tf_op jit(solution)/shard_map/ppermute | solution.py:29
  238.7 1.0 broadcast_select_fusion.2
  239.8 1.9 collective-permute-start.7
  241.7 359.8 %collective-permute-done.7 = f32[4,2,128,1024]{3,2,1,0:T(8,128)S(1)} collective-permute-done((f32[4,2,128,1024]{3,2,1,0:T(8,128)S(1)}, f32[4,2,128,1024]{3,2,1,0:T(8,128)S(1)}, u32[]{:S(2)}, u32[]{:S(2)}) %collective-permute-start.7) | collective-permute-done | bytes 4194336 | tf_op jit(solution)/shard_map/ppermute | solution.py:29
  601.6 2.9 broadcast_select_fusion.3
  604.5 1.9 collective-permute-start
  606.5 3.9 collective-permute-start.2
  610.4 4.0 collective-permute-start.1
  614.4 1.9 collective-permute-start.3
  623.7 25.6 %scatter_custom_fusion = f32[131072]{0:T(1024)S(1)} fusion(s32[4096]{0:T(1024)S(1)} %compare_select_fusion, f32[4096]{0:T(1024)S(1)} %fusion.86, f32[]{:T(128)} %constant.275.clone.1), kind=kCustom, calls=%fused_computation.148 | custom fusion | flops 4096 | bytes 524292 | tf_op jit(solution)/shard_map/scatter-add | solution.py:97
  649.6 50.2 %collective-permute-done.8 = f32[4,2,128,1024]{3,2,1,0:T(8,128)} collective-permute-done((f32[4,2,128,1024]{3,2,1,0:T(8,128)}, f32[4,2,128,1024]{3,2,1,0:T(8,128)}, u32[]{:S(2)}, u32[]{:S(2)}) %collective-permute-start.8) | collective-permute-done | bytes 4194336 | tf_op jit(solution)/shard_map/ppermute | solution.py:29
  699.9 4.6 broadcast_select_fusion.4
  704.5 1.9 collective-permute-start.10
  706.5 4.4 collective-permute-start.9
  710.9 4.8 fusion.41
  715.7 1.1 pad_maximum_fusion
  717.2 4.9 fusion.19
  722.9 4.8 fusion.16
  727.7 4.0 fusion.10
  732.5 3.8 fusion.13
  737.3 1.0 slice_add_fusion.1
  738.3 1.8 scatter-add.66
  740.1 0.9 slice_add_fusion
  741.0 1.6 scatter-add.67
  742.6 1.3 fusion.107
  744.2 1.0 slice_add_fusion.3
  745.3 1.8 scatter-add.51
  748.0 1.6 scatter-add.54
  749.6 5.9 fusion.52
  755.5 5.4 fusion.77
  760.9 3.9 fusion.54
  764.9 3.8 fusion.79
  770.0 4.9 fusion.57
  774.9 4.9 fusion.81
  781.3 4.0 fusion.75
  785.3 3.6 fusion.62
  788.9 2.6 maximum_bitcast_fusion.10
  791.5 2.4 maximum_bitcast_fusion.11
  794.0 5.0 fusion.83
  798.9 18.0 %psum.7 = f32[2,4]{1,0:T(2,128)S(1)} all-reduce(f32[2,4]{1,0:T(2,128)S(1)} %pad_maximum_fusion.5), channel_id=1, replica_groups=mesh['order'=32,'slab'=8] {'slab'}, use_global_device_ids=true, to_apply=%region_13.14 | all-reduce | flops 8 | bytes 64 | tf_op jit(solution)/shard_map/psum | solution.py:140
  818.8 3.5 fusion.47
  (111 shorter events, 13.0 us)
Async XLA Ops:
  0.6 52.4 %copy-start.3 = (f32[1,2,128,1024]{3,2,1,0:T(8,128)S(1)}, f32[1,2,128,1024]{3,2,1,0:T(8,128)}, u32[]{:S(2)}) copy-start(f32[1,2,128,1024]{3,2,1,0:T(8,128)} %param.29) | copy-start | bytes 3145732
  0.6 2.0 copy-start.10
  2.6 50.4 %collective-permute-start.4 = (f32[4,2,128,1024]{3,2,1,0:T(8,128)S(1)}, f32[4,2,128,1024]{3,2,1,0:T(8,128)S(1)}, u32[]{:S(2)}, u32[]{:S(2)}) collective-permute-start(f32[4,2,128,1024]{3,2,1,0:T(8,128)S(1)} %stack.114), channel_id=1, source_target_pairs={{248,0},{0,8},{8,16},{16,24},{24,32},{32,40},{40,48},{48,56},{56,6... | collective-permute-start | bytes 12582920 | tf_op jit(solution)/shard_map/ppermute | solution.py:29
  53.9 92.3 %collective-permute-start.5 = (f32[4,2,128,1024]{3,2,1,0:T(8,128)S(1)}, f32[4,2,128,1024]{3,2,1,0:T(8,128)S(1)}, u32[]{:S(2)}, u32[]{:S(2)}) collective-permute-start(f32[4,2,128,1024]{3,2,1,0:T(8,128)S(1)} %broadcast_select_fusion), channel_id=1, source_target_pairs={{240,0},{248,8},{0,16},{8,24},{16,32},{24,40},{32,48},{40,56},{48,... | collective-permute-start | bytes 12582920 | tf_op jit(solution)/shard_map/ppermute | solution.py:29
  147.8 91.0 %collective-permute-start.6 = (f32[4,2,128,1024]{3,2,1,0:T(8,128)S(1)}, f32[4,2,128,1024]{3,2,1,0:T(8,128)S(1)}, u32[]{:S(2)}, u32[]{:S(2)}) collective-permute-start(f32[4,2,128,1024]{3,2,1,0:T(8,128)S(1)} %broadcast_select_fusion.1), channel_id=1, source_target_pairs={{224,0},{232,8},{240,16},{248,24},{0,32},{8,40},{16,48},{24,56},{3... | collective-permute-start | bytes 12582920 | tf_op jit(solution)/shard_map/ppermute | solution.py:29
  239.8 361.8 %collective-permute-start.7 = (f32[4,2,128,1024]{3,2,1,0:T(8,128)S(1)}, f32[4,2,128,1024]{3,2,1,0:T(8,128)S(1)}, u32[]{:S(2)}, u32[]{:S(2)}) collective-permute-start(f32[4,2,128,1024]{3,2,1,0:T(8,128)S(1)} %broadcast_select_fusion.2), channel_id=1, source_target_pairs={{192,0},{200,8},{208,16},{216,24},{224,32},{232,40},{240,48},{248,... | collective-permute-start | bytes 12582920 | tf_op jit(solution)/shard_map/ppermute | solution.py:29
  601.6 3.0 copy-start.7
  601.6 15.4 %copy-start.20 = (f32[32]{0:T(128)S(1)}, f32[32]{0:T(128)}, u32[]{:S(2)}) copy-start(f32[32]{0:T(128)} %param.34) | copy-start | bytes 388
  601.6 15.4 %copy-start.21 = (f32[32]{0:T(128)S(1)}, f32[32]{0:T(128)}, u32[]{:S(2)}) copy-start(f32[32]{0:T(128)} %param.33) | copy-start | bytes 388
  601.6 18.1 %copy-start.8 = (s32[4096]{0:T(1024)S(1)}, s32[4096]{0:T(1024)}, u32[]{:S(2)}) copy-start(s32[4096]{0:T(1024)} %param.35) | copy-start | bytes 49156
  601.6 18.1 %copy-start.9 = (f32[4096]{0:T(1024)S(1)}, f32[4096]{0:T(1024)}, u32[]{:S(2)}) copy-start(f32[4096]{0:T(1024)} %param.36) | copy-start | bytes 49156
  604.5 95.3 %collective-permute-start.8 = (f32[4,2,128,1024]{3,2,1,0:T(8,128)}, f32[4,2,128,1024]{3,2,1,0:T(8,128)}, u32[]{:S(2)}, u32[]{:S(2)}) collective-permute-start(f32[4,2,128,1024]{3,2,1,0:T(8,128)} %broadcast_select_fusion.3), channel_id=1, source_target_pairs={{128,0},{136,8},{144,16},{152,24},{160,32},{168,40},{176,48},{184,... | collective-permute-start | bytes 12582920 | tf_op jit(solution)/shard_map/ppermute | solution.py:29
  604.5 44.9 %collective-permute-start = (f32[1,1024]{1,0:T(1,128)S(1)}, f32[1,1024]{1,0:T(1,128)S(1)}, u32[]{:S(2)}, u32[]{:S(2)}) collective-permute-start(f32[1,1024]{1,0:T(1,128)S(1)} %get-tuple-element.192), channel_id=1, source_target_pairs={{1,0},{2,1},{3,2},{4,3},{5,4},{6,5},{7,6},{9,8},{10,9},{11,10},{12... | collective-permute-start | bytes 12296 | tf_op jit(solution)/shard_map/ppermute | solution.py:19
  606.5 43.0 %collective-permute-start.2 = (f32[1,1024]{1,0:T(1,128)S(1)}, f32[1,1024]{1,0:T(1,128)S(1)}, u32[]{:S(2)}, u32[]{:S(2)}) collective-permute-start(f32[1,1024]{1,0:T(1,128)S(1)} %get-tuple-element.193), channel_id=1, source_target_pairs={{0,1},{1,2},{2,3},{3,4},{4,5},{5,6},{6,7},{8,9},{9,10},{10,11},{11... | collective-permute-start | bytes 12296 | tf_op jit(solution)/shard_map/ppermute | solution.py:17
  610.4 100.5 %collective-permute-start.1 = (f32[2,1,1024]{2,1,0:T(1,128)S(1)}, f32[2,1,1024]{2,1,0:T(1,128)S(1)}, u32[]{:S(2)}, u32[]{:S(2)}) collective-permute-start(f32[2,1,1024]{2,1,0:T(1,128)S(1)} %get-tuple-element.188), channel_id=1, source_target_pairs={{1,0},{2,1},{3,2},{4,3},{5,4},{6,5},{7,6},{9,8},{10,9},{11,10},{12... | collective-permute-start | bytes 24584 | tf_op jit(solution)/shard_map/ppermute | solution.py:19
  614.4 96.4 %collective-permute-start.3 = (f32[2,1,1024]{2,1,0:T(1,128)S(1)}, f32[2,1,1024]{2,1,0:T(1,128)S(1)}, u32[]{:S(2)}, u32[]{:S(2)}) collective-permute-start(f32[2,1,1024]{2,1,0:T(1,128)S(1)} %get-tuple-element.189), channel_id=1, source_target_pairs={{0,1},{1,2},{2,3},{3,4},{4,5},{5,6},{6,7},{8,9},{9,10},{10,11},{11... | collective-permute-start | bytes 24584 | tf_op jit(solution)/shard_map/ppermute | solution.py:17
  699.9 11.0 %copy-start = (f32[1024,1024]{1,0:T(8,128)S(1)}, f32[1024,1024]{1,0:T(8,128)}, u32[]{:S(2)}) copy-start(f32[1024,1024]{1,0:T(8,128)} %param.32) | copy-start | bytes 12582916
  704.5 11.3 %copy-start.1 = (f32[4,2,128,1024]{3,2,1,0:T(8,128)}, f32[4,2,128,1024]{3,2,1,0:T(8,128)S(1)}, u32[]{:S(2)}) copy-start(f32[4,2,128,1024]{3,2,1,0:T(8,128)S(1)} %broadcast_select_fusion.4) | copy-start | bytes 12582916
  704.5 11.2 %collective-permute-start.10 = (f32[4,2,1,1024]{3,2,1,0:T(1,128)S(1)}, f32[4,2,1,1024]{3,2,1,0:T(1,128)S(1)}, u32[]{:S(2)}, u32[]{:S(2)}) collective-permute-start(f32[4,2,1,1024]{3,2,1,0:T(1,128)S(1)} %get-tuple-element.181), channel_id=1, source_target_pairs={{1,0},{2,1},{3,2},{4,3},{5,4},{6,5},{7,6},{9,8},{10,9},{11,10},{12... | collective-permute-start | bytes 98312 | tf_op jit(solution)/shard_map/ppermute | solution.py:19
  706.5 9.3 %collective-permute-start.9 = (f32[4,2,1,1024]{3,2,1,0:T(1,128)S(1)}, f32[4,2,1,1024]{3,2,1,0:T(1,128)S(1)}, u32[]{:S(2)}, u32[]{:S(2)}) collective-permute-start(f32[4,2,1,1024]{3,2,1,0:T(1,128)S(1)} %get-tuple-element.180), channel_id=1, source_target_pairs={{0,1},{1,2},{2,3},{3,4},{4,5},{5,6},{6,7},{8,9},{9,10},{10,11},{11... | collective-permute-start | bytes 98312 | tf_op jit(solution)/shard_map/ppermute | solution.py:17
  749.6 11.3 %copy-start.2 = (f32[4,2,128,1024]{3,2,1,0:T(8,128)S(1)}, f32[4,2,128,1024]{3,2,1,0:T(8,128)}, u32[]{:S(2)}) copy-start(f32[4,2,128,1024]{3,2,1,0:T(8,128)} %copy-done.1) | copy-start | bytes 12582916
  749.6 11.3 %copy-start.4 = (f32[2,128,1024]{2,1,0:T(8,128)S(1)}, f32[2,128,1024]{2,1,0:T(8,128)}, u32[]{:S(2)}) copy-start(f32[2,128,1024]{2,1,0:T(8,128)} %scatter-add.54) | copy-start | bytes 3145732
  760.9 7.8 copy-start.18
  760.9 7.8 copy-start.19
  760.9 7.9 copy-start.16
  760.9 7.9 copy-start.17
  769.1 10.7 %copy-start.14 = (f32[1,128]{1,0:T(1,128)S(1)}, f32[1,128]{1,0:T(1,128)}, u32[]{:S(2)}) copy-start(f32[1,128]{1,0:T(1,128)} %get-tuple-element.235) | copy-start | bytes 1540
  769.1 10.7 %copy-start.15 = (f32[1,128]{1,0:T(1,128)S(1)}, f32[1,128]{1,0:T(1,128)}, u32[]{:S(2)}) copy-start(f32[1,128]{1,0:T(1,128)} %get-tuple-element.237) | copy-start | bytes 1540
  769.2 10.8 %copy-start.12 = (f32[1,128]{1,0:T(1,128)S(1)}, f32[1,128]{1,0:T(1,128)}, u32[]{:S(2)}) copy-start(f32[1,128]{1,0:T(1,128)} %get-tuple-element.234) | copy-start | bytes 1540
  769.2 10.8 %copy-start.13 = (f32[1,128]{1,0:T(1,128)S(1)}, f32[1,128]{1,0:T(1,128)}, u32[]{:S(2)}) copy-start(f32[1,128]{1,0:T(1,128)} %get-tuple-element.236) | copy-start | bytes 1540
  785.3 32.3 %copy-start.11 = (f32[1,128]{1,0:T(1,128)S(1)}, f32[1,128]{1,0:T(1,128)}, u32[]{:S(2)}) copy-start(f32[1,128]{1,0:T(1,128)} %get-tuple-element.233) | copy-start | bytes 1540
  785.3 32.6 %copy-start.5 = (f32[2,128,1024]{2,1,0:T(8,128)S(1)}, f32[2,128,1024]{2,1,0:T(8,128)}, u32[]{:S(2)}) copy-start(f32[2,128,1024]{2,1,0:T(8,128)} %fusion.41) | copy-start | bytes 3145732
  785.3 33.5 %copy-start.6 = (f32[1,128,1024]{2,1,0:T(8,128)S(1)}, f32[1,128,1024]{2,1,0:T(8,128)}, u32[]{:S(2)}) copy-start(f32[1,128,1024]{2,1,0:T(8,128)} %get-tuple-element.168) | copy-start | bytes 1572868
where the time goes:
time: 832 us; the launch traced here: 823 us
  waiting for transfers between devices  638 us (77%)
  other arithmetic  95.1 us (11%)
  starting transfers between devices  25.8 us (3%)
  matrix products  22.3 us (3%)
  local copies, waits for them, and re-layouts  18.4 us (2%)
  blocking collectives  18 us (2%)
    ppermute x5, waiting for transfers between devices, passed_along(): return lax.ppermute(block, axis, route)  638 us
    add x6, other arithmetic, make_term(): temp_re * helm[0] - temp_im * helm[1]  28 us
    scatter-add x1, other arithmetic, local(): jnp.zeros((layers * width,), jnp.float32)  25.6 us
    dot_general x5, matrix products, apply_padded(): jnp.einsum('cxz,zw->cxw', center, transverse, precision=lax.Precision.HIG...  22.3 us
    psum x1, blocking collectives, local(): whole_sums = lax.psum(partial_sums, 'slab')  18 us
  transfers between devices with their start and end apart: 11, of which 5 were waited for; matrix products, arithmetic and copies ran while one was open for 5% of the time, Pallas kernels for 0%

commit v1 on v0

v1 whole, which is shorter than its diff:
```python
import functools
import math

import jax
import jax.numpy as jnp
from jax import lax
from jax.experimental import pallas as pl
from jax.experimental.pallas import tpu as pltpu
from jax.sharding import PartitionSpec as P

MESH = pl.DeviceIdType.MESH
EARLY = 10


def kernel(
    orders,
    slabs,
    scale,
    direct_ref,
    adjoint_ref,
    sound_hbm,
    transverse_hbm,
    temp_ref,
    gain_ref,
    cells_ref,
    weight_ref,
    offsets_ref,
    image_ref,
    coupling_ref,
    dstage,
    astage,
    istage,
    field,
    adj,
    arrived,
    base,
    flamed,
    field_hi,
    field_lo,
    tmat,
    tmat_hi,
    tmat_lo,
    sound_pad,
    halo_send,
    halo_recv,
    turn_cos,
    turn_sin,
    csend,
    cpart,
    cslab,
    local_sem,
    send_sem,
    recv_sem,
):
    me = lax.axis_index("order")
    slab = lax.axis_index("slab")
    layers, width = direct_ref.shape[1], direct_ref.shape[2]
    rows = layers // orders
    last = width - 128
    offs = offsets_ref.shape[0]
    f32, bf16 = jnp.float32, jnp.bfloat16

    def order_dev(which):
        return {"order": which}

    def peer(step):
        return lax.rem(me + step, orders)

    fetch_t = pltpu.make_async_copy(transverse_hbm, tmat, local_sem.at[0])
    fetch_t.start()
    fetch_c = pltpu.make_async_copy(
        sound_hbm, sound_pad.at[pl.ds(8, layers)], local_sem.at[1]
    )
    fetch_c.start()

    barrier = pltpu.get_barrier_semaphore()

    def greet_order(step, carry):
        pl.semaphore_signal(
            barrier, inc=1, device_id=order_dev(peer(step)), device_id_type=MESH
        )
        return carry

    def greet_slab(step, carry):
        pl.semaphore_signal(
            barrier,
            inc=1,
            device_id={"slab": lax.rem(slab + step, slabs)},
            device_id_type=MESH,
        )
        return carry

    has_above_slab = jnp.logical_and(me == 0, slab > 0)
    has_below_slab = jnp.logical_and(me == orders - 1, slab < slabs - 1)
    has_above = jnp.logical_or(me > 0, slab > 0)
    has_below = jnp.logical_or(me < orders - 1, slab < slabs - 1)
    above_dev = {
        "order": lax.rem(me + orders - 1, orders),
        "slab": lax.rem(slab + slabs - lax.div(orders - me, orders), slabs),
    }
    below_dev = {
        "order": lax.rem(me + 1, orders),
        "slab": lax.rem(slab + lax.div(me + 1, orders), slabs),
    }
    lax.fori_loop(1, orders, greet_order, 0)
    lax.fori_loop(1, slabs, greet_slab, 0)

    @pl.when(has_above_slab)
    def _():
        pl.semaphore_signal(barrier, inc=1, device_id=above_dev, device_id_type=MESH)

    @pl.when(has_below_slab)
    def _():
        pl.semaphore_signal(barrier, inc=1, device_id=below_dev, device_id_type=MESH)

    sub = lax.broadcasted_iota(jnp.int32, (8, 128), 0)
    lane = lax.broadcasted_iota(jnp.int32, (8, 128), 1)
    sub_w = lax.broadcasted_iota(jnp.int32, (8, width), 0)

    def pack(source, stage):
        def body(tile, carry):
            at = pl.multiple_of(tile * 8, 8)
            re = source[0, pl.ds(at, 8), :]
            im = source[1, pl.ds(at, 8), :]
            stage[2 * tile] = jnp.where(sub_w < 4, re, pltpu.roll(im, 4, 0))
            stage[2 * tile + 1] = jnp.where(sub_w < 4, pltpu.roll(re, 4, 0), im)
            return carry

        lax.fori_loop(0, layers // 8, body, 0)

    pack(direct_ref, dstage)

    extra = has_above_slab.astype(jnp.int32) + has_below_slab.astype(jnp.int32)
    pl.semaphore_wait(barrier, orders - 1 + slabs - 1 + extra)

    def scatter_copy(stage, into, sem, step):
        to = peer(step)
        return pltpu.make_async_remote_copy(
            src_ref=stage.at[to],
            dst_ref=into.at[me],
            send_sem=send_sem.at[sem],
            recv_sem=recv_sem.at[sem],
            device_id=order_dev(to),
            device_id_type=MESH,
        )

    def scatter(stage, into, sem, first, end):
        def body(step, carry):
            scatter_copy(stage, into, sem, step).start()
            return carry

        lax.fori_loop(first, end, body, 0)

    def wait_bytes(ref, sem):
        pltpu.make_async_copy(ref, ref, sem).wait()

    def others(ref):
        return ref.at[pl.ds(0, orders - 1)]

    scatter(dstage, field, 0, 1, orders)
    field[me] = dstage[me]

    fetch_c.wait()

    def sound_up():
        return pltpu.make_async_remote_copy(
            src_ref=sound_pad.at[pl.ds(8, 8)],
            dst_ref=sound_pad.at[pl.ds(8 + layers, 8)],
            send_sem=send_sem.at[3],
            recv_sem=recv_sem.at[3],
            device_id={"slab": lax.rem(slab + slabs - 1, slabs)},
            device_id_type=MESH,
        )

    def sound_down():
        return pltpu.make_async_remote_copy(
            src_ref=sound_pad.at[pl.ds(layers, 8)],
            dst_ref=sound_pad.at[pl.ds(0, 8)],
            send_sem=send_sem.at[4],
            recv_sem=recv_sem.at[4],
            device_id={"slab": lax.rem(slab + 1, slabs)},
            device_id_type=MESH,
        )

    @pl.when(slab > 0)
    def _():
        sound_up().start()

    @pl.when(slab < slabs - 1)
    def _():
        sound_down().start()

    pack(adjoint_ref, astage)
    scatter(astage, adj, 1, 1, EARLY)
    adj[me] = astage[me]

    bin_ids = lax.broadcasted_iota(jnp.int32, (1, temp_ref.shape[1]), 1)
    tau_re, tau_im, gain_re, gain_im = [], [], [], []
    for j in range(offs):
        turns = lax.rem(offsets_ref[j] * bin_ids, orders)
        angles = 2.0 * math.pi / orders * turns.astype(f32)
        cos, sin = jnp.cos(angles), jnp.sin(angles)
        tau_re.append(jnp.sum(temp_ref[...] * cos) * (1.0 / orders))
        tau_im.append(-jnp.sum(temp_ref[...] * sin) * (1.0 / orders))
        gain_re.append(jnp.sum(gain_ref[...] * cos) * (1.0 / orders))
        gain_im.append(-jnp.sum(gain_ref[...] * sin) * (1.0 / orders))

    def turn_table(source, carry):
        angle = jnp.full((8, 128), 2.0 * math.pi / orders, f32) * source.astype(f32)
        turn_cos[source] = jnp.cos(angle)
        turn_sin[source] = jnp.where(sub < 4, -1.0, 1.0) * jnp.sin(angle)
        return carry

    lax.fori_loop(0, orders, turn_table, 0)

    first_cell = (slab * layers + me * rows) * width
    flame_step = 512
    flames = cells_ref.shape[1]
    sub_f = lax.broadcasted_iota(jnp.int32, (8, flame_step), 0)
    sub_c = lax.broadcasted_iota(jnp.int32, (width, flame_step), 0)

    def place(step, total):
        at = pl.multiple_of(step * flame_step, flame_step)
        ids = cells_ref[:, pl.ds(at, flame_step)] - first_cell
        weights = weight_ref[:, pl.ds(at, flame_step)]
        row = ids >> (width.bit_length() - 1)
        column = ids & (width - 1)
        mine = row == (sub_f & (rows - 1))
        spread = jnp.where(mine, weights, 0.0)
        hi = spread.astype(bf16)
        rest = spread - hi.astype(f32)
        mid = rest.astype(bf16)
        low = (rest - mid.astype(f32)).astype(bf16)
        pick = jnp.where(sub_c == column, 1.0, 0.0).astype(bf16)
        left = jnp.concatenate([hi.astype(f32), mid.astype(f32), low.astype(f32)], axis=0)
        part = lax.dot_general(
            left.astype(bf16), pick, (((1,), (1,)), ((), ())), preferred_element_type=f32
        )
        return total + (part[0:8] + part[8:16] + part[16:24])

    flame = lax.fori_loop(
        0, flames // flame_step, place, jnp.zeros((8, width), f32)
    )

    fetch_t.wait()

    def halves(block, carry):
        at = pl.ds(pl.multiple_of(block * 32, 32), 32)
        value = tmat[at, :]
        hi = value.astype(bf16)
        tmat_hi[at, :] = hi
        tmat_lo[at, :] = (value - hi.astype(f32)).astype(bf16)
        return carry

    lax.fori_loop(0, width // 32, halves, 0)

    @pl.when(slab < slabs - 1)
    def _():
        sound_up().wait_recv()

    @pl.when(slab > 0)
    def _():
        sound_down().wait_recv()

    @pl.when(slab < slabs - 1)
    def _():
        sound_down().wait_send()

    @pl.when(slab > 0)
    def _():
        sound_up().wait_send()

    @pl.when(slab == slabs - 1)
    def _():
        sound_pad[pl.ds(8 + layers, 8)] = jnp.zeros((8, width), f32)

    @pl.when(slab == 0)
    def _():
        sound_pad[pl.ds(0, 8)] = jnp.zeros((8, width), f32)

    tile = lax.div(me, 2)
    odd = lax.rem(me, 2) == 1
    top = sound_pad[pl.ds(pl.multiple_of(tile * 8, 8), 8), :]
    middle = sound_pad[pl.ds(pl.multiple_of(tile * 8 + 8, 8), 8), :]
    bottom = sound_pad[pl.ds(pl.multiple_of(tile * 8 + 16, 8), 8), :]
    low_half = sub_w < 4
    top_turned = pltpu.roll(top, 4, 0)
    middle_turned = pltpu.roll(middle, 4, 0)
    bottom_turned = pltpu.roll(bottom, 4, 0)
    own4 = jnp.where(odd, jnp.where(low_half, middle_turned, middle), jnp.where(low_half, middle, middle_turned))
    before = jnp.where(odd, middle, pltpu.roll(top, 4, 0))
    after = jnp.where(odd, bottom, middle_turned)
    above_row = jnp.where(low_half, pltpu.roll(before, 5, 0), pltpu.roll(before, 1, 0))
    below_row = jnp.where(low_half, pltpu.roll(after, 3, 0), pltpu.roll(after, 7, 0))
    place_in = sub_w & 3
    sound_above = jnp.where(place_in == 0, above_row, pltpu.roll(own4, 1, 0))
    sound_below = jnp.where(place_in == 3, below_row, pltpu.roll(own4, 7, 0))
    coef_below = 0.5 * (own4 + sound_below)
    coef_above = 0.5 * (own4 + sound_above)
    seam_first = 0.5 * (own4[:, 0:128] + pltpu.roll(own4[:, last:], 1, 1))
    seam_last = 0.5 * (own4[:, last:] + pltpu.roll(own4[:, 0:128], 127, 1))
    is_first = lane == 0
    is_last = lane == 127
    sign = jnp.where(sub < 4, -1.0, 1.0)
    sign_w = jnp.where(sub_w < 4, -1.0, 1.0)

    wait_bytes(others(field), recv_sem.at[0])

    def edges(group, carry):
        low = jnp.zeros((8, width), f32)
        high = jnp.zeros((8, width), f32)
        for i in range(4):
            value = field[4 * group + i]
            low = jnp.where(sub_w == 2 * i, pltpu.roll(value, (2 * i) % 8, 0), low)
            low = jnp.where(sub_w == 2 * i + 1, pltpu.roll(value, (2 * i + 5) % 8, 0), low)
            high = jnp.where(sub_w == 2 * i, pltpu.roll(value, (2 * i + 5) % 8, 0), high)
            high = jnp.where(sub_w == 2 * i + 1, pltpu.roll(value, (2 * i + 2) % 8, 0), high)
        at = pl.ds(pl.multiple_of(group * 8, 8), 8)
        halo_send[0, at, :] = low
        halo_send[1, at, :] = high
        return carry

    lax.fori_loop(0, orders // 4, edges, 0)

    def halo_up():
        return pltpu.make_async_remote_copy(
            src_ref=halo_send.at[0],
            dst_ref=halo_recv.at[1],
            send_sem=send_sem.at[5],
            recv_sem=recv_sem.at[5],
            device_id=above_dev,
            device_id_type=MESH,
        )

    def halo_down():
        return pltpu.make_async_remote_copy(
            src_ref=halo_send.at[1],
            dst_ref=halo_recv.at[0],
            send_sem=send_sem.at[6],
            recv_sem=recv_sem.at[6],
            device_id=below_dev,
            device_id_type=MESH,
        )

    @pl.when(has_above)
    def _():
        halo_up().start()

    @pl.when(has_below)
    def _():
        halo_down().start()

    scatter(astage, adj, 1, EARLY, orders)

    def split(group, carry):
        value = field[pl.ds(4 * group, 4)].reshape(32, width)
        at = pl.ds(pl.multiple_of(group * 32, 32), 32)
        hi = value.astype(bf16)
        field_hi[at, :] = hi
        field_lo[at, :] = (value - hi.astype(f32)).astype(bf16)
        return carry

    lax.fori_loop(0, orders // 4, split, 0)

    def across(block, carry):
        at = pl.ds(pl.multiple_of(block * 256, 256), 256)
        dot = functools.partial(jnp.dot, preferred_element_type=f32)
        t_hi = tmat_hi[:, at]
        t_lo = tmat_lo[:, at]
        hi = field_hi[...]
        product = dot(hi, t_lo) + dot(field_lo[...], t_hi) + dot(hi, t_hi)
        base[:, :, at] = product.reshape(orders, 8, 256)
        return carry

    lax.fori_loop(0, width // 256, across, 0)

    @pl.when(has_below)
    def _():
        halo_up_recv = halo_up()
        halo_up_recv.wait_recv()

    @pl.when(has_above)
    def _():
        halo_down_recv = halo_down()
        halo_down_recv.wait_recv()

    @pl.when(jnp.logical_not(has_below))
    def _():
        halo_recv[1] = jnp.zeros((2 * orders, width), f32)

    @pl.when(jnp.logical_not(has_above))
    def _():
        halo_recv[0] = jnp.zeros((2 * orders, width), f32)

    def helm(group, carry):
        at = pl.ds(pl.multiple_of(group * 8, 8), 8)
        upper = halo_recv[0, at, :]
        lower = halo_recv[1, at, :]
        for i in range(4):
            source = 4 * group + i
            value = field[source]
            up = jnp.where(
                sub_w == 0, pltpu.roll(upper, (8 - 2 * i) % 8, 0), pltpu.roll(value, 1, 0)
            )
            up = jnp.where(sub_w == 4, pltpu.roll(upper, (11 - 2 * i) % 8, 0), up)
            down = jnp.where(
                sub_w == 3, pltpu.roll(lower, (11 - 2 * i) % 8, 0), pltpu.roll(value, 7, 0)
            )
            down = jnp.where(sub_w == 7, pltpu.roll(lower, (14 - 2 * i) % 8, 0), down)
            axial = coef_below * (value - down) + coef_above * (value - up)
            base[source] = base[source] + axial
            flamed[source] = flame * value
            cos, sin = turn_cos[source], turn_sin[source]
            head, tail = value[:, 0:128], value[:, last:]
            tail_here = pltpu.roll(tail, 1, 1)
            head_here = pltpu.roll(head, 127, 1)
            behind = cos * tail_here - sin * pltpu.roll(tail_here, 4, 0)
            ahead = cos * head_here + sin * pltpu.roll(head_here, 4, 0)
            base[source, :, 0:128] = base[source, :, 0:128] + jnp.where(
                is_first, seam_first * (head - behind), 0.0
            )
            base[source, :, last:] = base[source, :, last:] + jnp.where(
                is_last, seam_last * (tail - ahead), 0.0
            )
        return carry

    lax.fori_loop(0, orders // 4, helm, 0)

    def mixed(target):
        plain = base[target]
        turned = jnp.zeros((8, width), f32)
        for j in range(offs):
            source = lax.rem(target - offsets_ref[j] + orders, orders)
            helm_src = base[source]
            flame_src = flamed[source]
            plain = plain + (helm_src * tau_re[j] + flame_src * gain_re[j])
            turned = turned + (helm_src * tau_im[j] + flame_src * gain_im[j])
        return plain + sign_w * pltpu.roll(turned, 4, 0)

    def give(step, carry):
        target = peer(step)
        istage[target] = mixed(target)
        scatter_copy(istage, arrived, 2, step).start()
        return carry

    lax.fori_loop(1, orders, give, 0)
    arrived[me] = mixed(me)

    wait_bytes(others(adj), recv_sem.at[1])
    row8 = lax.broadcasted_iota(jnp.int32, (8, 128), 0)

    def fold(value):
        total = value[:, 0:128]
        for block in range(1, width // 128):
            total = total + value[:, block * 128 : block * 128 + 128]
        return total

    def couple(target, carry):
        mine = adj[target]
        mine_turned = sign_w * pltpu.roll(mine, 4, 0)
        table = jnp.zeros((8, 128), f32)
        for j in range(offs):
            source = lax.rem(target - offsets_ref[j] + orders, orders)
            helm_src = base[source]
            flame_src = flamed[source]
            same = fold(mine * helm_src)
            cross = fold(mine_turned * helm_src)
            flame_same = fold(mine * flame_src)
            flame_cross = fold(mine_turned * flame_src)
            part_re = (
                tau_re[j] * same - tau_im[j] * cross
                + gain_re[j] * flame_same - gain_im[j] * flame_cross
            )
            part_im = (
                tau_re[j] * cross + tau_im[j] * same
                + gain_re[j] * flame_cross + gain_im[j] * flame_same
            )
            table = jnp.where(row8 == j, jnp.sum(part_re, axis=0, keepdims=True), table)
            table = jnp.where(
                row8 == offs + j, jnp.sum(part_im, axis=0, keepdims=True), table
            )
        column = jnp.sum(table, axis=1, keepdims=True)
        csend[target] = jnp.sum(
            jnp.where(lane == row8, column, 0.0), axis=0, keepdims=True
        )
        return carry

    lax.fori_loop(0, orders, couple, 0)
    scatter(csend, cpart, 7, 1, orders)
    cpart[me] = csend[me]
    wait_bytes(others(cpart), recv_sem.at[7])
    total = cpart[0]
    for k in range(1, orders):
        total = total + cpart[k]
    cslab[slab] = total

    def slab_copy(step):
        return pltpu.make_async_remote_copy(
            src_ref=cslab.at[slab],
            dst_ref=cslab.at[slab],
            send_sem=send_sem.at[8],
            recv_sem=recv_sem.at[8],
            device_id={"slab": lax.rem(slab + step, slabs)},
            device_id_type=MESH,
        )

    def slab_start(step, carry):
        slab_copy(step).start()
        return carry

    lax.fori_loop(1, slabs, slab_start, 0)

    wait_bytes(others(arrived), recv_sem.at[2])

    def unpack(tile_id, carry):
        at = pl.ds(pl.multiple_of(tile_id * 8, 8), 8)
        even = arrived[2 * tile_id]
        odd_tile = arrived[2 * tile_id + 1]
        image_ref[0, at, :] = jnp.where(low_half, even, pltpu.roll(odd_tile, 4, 0))
        image_ref[1, at, :] = jnp.where(low_half, pltpu.roll(even, 4, 0), odd_tile)
        return carry

    lax.fori_loop(0, layers // 8, unpack, 0)

    wait_bytes(cslab.at[pl.ds(0, slabs - 1)], recv_sem.at[8])
    whole = cslab[0]
    for k in range(1, slabs):
        whole = whole + cslab[k]
    whole = whole * scale
    coupling_ref[0:1, :] = whole[:, 0:offs]
    coupling_ref[1:2, :] = whole[:, offs : 2 * offs]

    wait_bytes(others(dstage), send_sem.at[0])
    wait_bytes(others(astage), send_sem.at[1])
    wait_bytes(others(istage), send_sem.at[2])
    wait_bytes(others(csend), send_sem.at[7])
    wait_bytes(cslab.at[pl.ds(0, slabs - 1)], send_sem.at[8])

    @pl.when(has_above)
    def _():
        halo_up().wait_send()

    @pl.when(has_below)
    def _():
        halo_down().wait_send()


def solution(mesh):
    orders = mesh.shape["order"]
    slabs = mesh.shape["slab"]

    def local(
        direct, adjoint, sound, transverse, burner_temp, burner_gain, flame_cells, flame_weight, offsets
    ):
        layers, width = direct.shape[2], direct.shape[3]
        offs = offsets.shape[0]
        f32, bf16 = jnp.float32, jnp.bfloat16
        vmem = pl.BlockSpec(memory_space=pltpu.VMEM)
        anywhere = pl.BlockSpec(memory_space=pl.ANY)
        block = (orders, 8, width)
        image, coupling = pl.pallas_call(
            functools.partial(
                kernel, orders, slabs, 1.0 / math.sqrt(layers * slabs * width)
            ),
            out_shape=(
                jax.ShapeDtypeStruct((2, layers, width), f32),
                jax.ShapeDtypeStruct((2, offs), f32),
            ),
            in_specs=[vmem, vmem, anywhere, anywhere, vmem, vmem, vmem, vmem]
            + [pl.BlockSpec(memory_space=pltpu.SMEM)],
            out_specs=(vmem, vmem),
            scratch_shapes=[
                pltpu.VMEM(block, f32),
                pltpu.VMEM(block, f32),
                pltpu.VMEM(block, f32),
                pltpu.VMEM(block, f32),
                pltpu.VMEM(block, f32),
                pltpu.VMEM(block, f32),
                pltpu.VMEM(block, f32),
                pltpu.VMEM(block, f32),
                pltpu.VMEM((orders * 8, width), bf16),
                pltpu.VMEM((orders * 8, width), bf16),
                pltpu.VMEM((width, width), f32),
                pltpu.VMEM((width, width), bf16),
                pltpu.VMEM((width, width), bf16),
                pltpu.VMEM((layers + 16, width), f32),
                pltpu.VMEM((2, 2 * orders, width), f32),
                pltpu.VMEM((2, 2 * orders, width), f32),
                pltpu.VMEM((orders, 8, 128), f32),
                pltpu.VMEM((orders, 8, 128), f32),
                pltpu.VMEM((orders, 1, 128), f32),
                pltpu.VMEM((orders, 1, 128), f32),
                pltpu.VMEM((slabs, 1, 128), f32),
                pltpu.SemaphoreType.DMA((2,)),
                pltpu.SemaphoreType.DMA((9,)),
                pltpu.SemaphoreType.DMA((9,)),
            ],
            compiler_params=pltpu.CompilerParams(
                collective_id=0, has_side_effects=True, vmem_limit_bytes=48 * 2**20
            ),
        )(
            direct[0],
            adjoint[0],
            sound,
            transverse,
            burner_temp[None],
            burner_gain[None],
            flame_cells[None],
            flame_weight[None],
            offsets,
        )
        return image[None], coupling[None]

    in_specs = (
        P("order", None, "slab", None),
        P("order", None, "slab", None),
        P("slab", None),
        P(),
        P(),
        P(),
        P(),
        P(),
        P(),
    )
    out_specs = (P("order", None, "slab", None), P("order", None, None))
    return jax.shard_map(local, mesh=mesh, in_specs=in_specs, out_specs=out_specs, check_vma=False)
```

time: 832 us -> 100 us (0.12)
  the two profiles are of different devices: /device:TPU:98 before, /device:TPU:1 now
where the time goes in v1:
time: 100 us; the launch traced here: 99.3 us
  Pallas kernels  90.2 us (90%)
  local copies, waits for them, and re-layouts  8.42 us (8%)
    pallas_call x1, Pallas kernels, local(): pl.pallas_call(functools.partial(kernel, orders, slabs, 1.0 / math.sqrt(l...  90.2 us
    unnamed x18, local copies, waits for them, and re-layouts  8.42 us

profile of v1, /device:TPU:1, one launch (start us, length us, event | category | flops | bytes accessed | tf_op | source)
XLA Modules:
  0.0 99.3 jit_solution(8627368347942673816)
XLA Ops:
  0.6 0.0 copy-start
  0.6 1.2 %copy-done = f32[1,2,128,1024]{3,2,1,0:T(8,128)S(1)} copy-done((f32[1,2,128,1024]{3,2,1,0:T(8,128)S(1)}, f32[1,2,128,1024]{3,2,1,0:T(8,128)}, u32[]{:S(2)}) %copy-start) | copy-done | bytes 1048600
  1.9 0.0 copy-start.1
  1.9 1.2 %copy-done.1 = f32[1,2,128,1024]{3,2,1,0:T(8,128)S(1)} copy-done((f32[1,2,128,1024]{3,2,1,0:T(8,128)S(1)}, f32[1,2,128,1024]{3,2,1,0:T(8,128)}, u32[]{:S(2)}) %copy-start.1) | copy-done | bytes 1048600
  3.1 0.0 copy-start.2
  3.1 1.0 %copy-done.2 = f32[128,1024]{1,0:T(8,128)S(1)} copy-done((f32[128,1024]{1,0:T(8,128)S(1)}, f32[128,1024]{1,0:T(8,128)}, u32[]{:S(2)}) %copy-start.2) | copy-done | bytes 524312
  4.1 0.0 copy-start.3
  4.1 0.7 copy-done.3
  4.8 0.0 copy-start.4
  4.8 0.7 copy-done.4
  5.6 0.0 copy-start.5
  5.6 0.7 copy-done.5
  6.2 0.0 copy-start.6
  6.2 0.7 copy-done.6
  6.9 0.0 copy-start.7
  6.9 0.7 copy-done.7
  7.5 90.2 %shard_map.104 = (f32[2,128,1024]{2,1,0:T(8,128)S(1)}, f32[2,4]{1,0:T(2,128)S(1)}) custom-call(f32[2,128,1024]{2,1,0:T(8,128)S(1)} %bitcast.9, f32[2,128,1024]{2,1,0:T(8,128)S(1)} %bitcast.10, f32[128,1024]{1,0:T(8,128)S(1)} %copy-done.2, f32[1024,1024]{1,0:T(8,128)} %transverse_hbm.1, f32[1,32]{1,0:T(1,128)S(1)} %bitcast.14, f32[1,32]{1,0:T(1,128)S(1)} %bitcast.15, ...), custom_call_target="tpu_custom_call" | custom-call | tf_op jit(solution)/shard_map/pallas_call | solution.py:561
  97.8 1.0 copy.13
  98.7 0.6 copy.14
Async XLA Ops:
  0.6 1.2 %copy-start = (f32[1,2,128,1024]{3,2,1,0:T(8,128)S(1)}, f32[1,2,128,1024]{3,2,1,0:T(8,128)}, u32[]{:S(2)}) copy-start(f32[1,2,128,1024]{3,2,1,0:T(8,128)} %param.9) | copy-start | bytes 3145732
  1.9 1.2 %copy-start.1 = (f32[1,2,128,1024]{3,2,1,0:T(8,128)S(1)}, f32[1,2,128,1024]{3,2,1,0:T(8,128)}, u32[]{:S(2)}) copy-start(f32[1,2,128,1024]{3,2,1,0:T(8,128)} %param.10) | copy-start | bytes 3145732
  3.1 1.0 %copy-start.2 = (f32[128,1024]{1,0:T(8,128)S(1)}, f32[128,1024]{1,0:T(8,128)}, u32[]{:S(2)}) copy-start(f32[128,1024]{1,0:T(8,128)} %sound_hbm.1) | copy-start | bytes 1572868
  4.1 0.7 copy-start.3
  4.8 0.7 copy-start.4
  5.6 0.7 copy-start.5
  6.2 0.7 copy-start.6
  6.9 0.7 copy-start.7

commit v2 on v1

--- a/solution.py
+++ b/solution.py
@@ -9,30 +9,39 @@
 from jax.sharding import PartitionSpec as P
 
 MESH = pl.DeviceIdType.MESH
-EARLY = 10
+STRIDE = 11
+EARLY = 20
+FIRST = 24
+SECOND = 30
 
 
 def kernel(
     orders,
     slabs,
     scale,
+    direct_hbm,
+    adjoint_hbm,
+    sound_hbm,
+    transverse_hbm,
+    temp_hbm,
+    gain_hbm,
+    cells_hbm,
+    weight_hbm,
+    offsets_hbm,
+    arrived,
+    coupling_hbm,
     direct_ref,
     adjoint_ref,
-    sound_hbm,
-    transverse_hbm,
     temp_ref,
     gain_ref,
     cells_ref,
     weight_ref,
     offsets_ref,
-    image_ref,
-    coupling_ref,
     dstage,
     astage,
     istage,
     field,
     adj,
-    arrived,
     base,
     flamed,
     field_hi,
@@ -48,6 +57,7 @@
     csend,
     cpart,
     cslab,
+    sums_ref,
     local_sem,
     send_sem,
     recv_sem,
@@ -64,14 +74,14 @@
         return {"order": which}
 
     def peer(step):
-        return lax.rem(me + step, orders)
-
-    fetch_t = pltpu.make_async_copy(transverse_hbm, tmat, local_sem.at[0])
-    fetch_t.start()
-    fetch_c = pltpu.make_async_copy(
-        sound_hbm, sound_pad.at[pl.ds(8, layers)], local_sem.at[1]
-    )
-    fetch_c.start()
+        return lax.rem(me + lax.rem(step * STRIDE, orders), orders)
+
+    def fetch(source, into, sem):
+        copy = pltpu.make_async_copy(source, into, local_sem.at[sem])
+        copy.start()
+        return copy
+
+    fetch_d = fetch(direct_hbm, direct_ref, 2)
 
     barrier = pltpu.get_barrier_semaphore()
 
@@ -128,6 +138,17 @@
 
         lax.fori_loop(0, layers // 8, body, 0)
 
+    fetch_c = fetch(sound_hbm, sound_pad.at[pl.ds(8, layers)], 1)
+    fetch_a = fetch(adjoint_hbm, adjoint_ref, 3)
+    small = [
+        fetch(offsets_hbm, offsets_ref, 4),
+        fetch(temp_hbm, temp_ref, 5),
+        fetch(gain_hbm, gain_ref, 6),
+        fetch(cells_hbm, cells_ref, 7),
+        fetch(weight_hbm, weight_ref, 8),
+    ]
+    fetch_t = fetch(transverse_hbm, tmat, 0)
+    fetch_d.wait()
     pack(direct_ref, dstage)
 
     extra = has_above_slab.astype(jnp.int32) + has_below_slab.astype(jnp.int32)
@@ -190,10 +211,13 @@
     def _():
         sound_down().start()
 
+    fetch_a.wait()
     pack(adjoint_ref, astage)
     scatter(astage, adj, 1, 1, EARLY)
     adj[me] = astage[me]
 
+    for copy in small:
+        copy.wait()
     bin_ids = lax.broadcasted_iota(jnp.int32, (1, temp_ref.shape[1]), 1)
     tau_re, tau_im, gain_re, gain_im = [], [], [], []
     for j in range(offs):
@@ -443,8 +467,7 @@
         scatter_copy(istage, arrived, 2, step).start()
         return carry
 
-    lax.fori_loop(1, orders, give, 0)
-    arrived[me] = mixed(me)
+    lax.fori_loop(1, FIRST, give, 0)
 
     wait_bytes(others(adj), recv_sem.at[1])
     row8 = lax.broadcasted_iota(jnp.int32, (8, 128), 0)
@@ -488,6 +511,7 @@
     lax.fori_loop(0, orders, couple, 0)
     scatter(csend, cpart, 7, 1, orders)
     cpart[me] = csend[me]
+    lax.fori_loop(FIRST, SECOND, give, 0)
     wait_bytes(others(cpart), recv_sem.at[7])
     total = cpart[0]
     for k in range(1, orders):
@@ -510,26 +534,23 @@
 
     lax.fori_loop(1, slabs, slab_start, 0)
 
-    wait_bytes(others(arrived), recv_sem.at[2])
-
-    def unpack(tile_id, carry):
-        at = pl.ds(pl.multiple_of(tile_id * 8, 8), 8)
-        even = arrived[2 * tile_id]
-        odd_tile = arrived[2 * tile_id + 1]
-        image_ref[0, at, :] = jnp.where(low_half, even, pltpu.roll(odd_tile, 4, 0))
-        image_ref[1, at, :] = jnp.where(low_half, pltpu.roll(even, 4, 0), odd_tile)
-        return carry
-
-    lax.fori_loop(0, layers // 8, unpack, 0)
-
+    lax.fori_loop(SECOND, orders, give, 0)
+    istage[me] = mixed(me)
+    keep = pltpu.make_async_copy(istage.at[me], arrived.at[me], local_sem.at[9])
+    keep.start()
     wait_bytes(cslab.at[pl.ds(0, slabs - 1)], recv_sem.at[8])
     whole = cslab[0]
     for k in range(1, slabs):
         whole = whole + cslab[k]
     whole = whole * scale
-    coupling_ref[0:1, :] = whole[:, 0:offs]
-    coupling_ref[1:2, :] = whole[:, offs : 2 * offs]
-
+    sums_ref[0:1, :] = whole[:, 0:offs]
+    sums_ref[1:2, :] = whole[:, offs : 2 * offs]
+    give_sums = pltpu.make_async_copy(sums_ref, coupling_hbm, local_sem.at[10])
+    give_sums.start()
+    keep.wait()
+    give_sums.wait()
+
+    wait_bytes(others(arrived), recv_sem.at[2])
     wait_bytes(others(dstage), send_sem.at[0])
     wait_bytes(others(astage), send_sem.at[1])
     wait_bytes(others(istage), send_sem.at[2])
@@ -543,6 +564,46 @@
     @pl.when(has_below)
     def _():
         halo_down().wait_send()
+
+
+def write_out(arrived_hbm, sums_hbm, image_hbm, coupling_hbm, arrived, image, sem):
+    layers, width = image.shape[1], image.shape[2]
+    low_half = lax.broadcasted_iota(jnp.int32, (8, width), 0) < 4
+    pieces = 4
+    part = layers // pieces
+    blocks = arrived.shape[0] // pieces
+
+    def pull(piece):
+        at = pl.ds(piece * blocks, blocks)
+        return pltpu.make_async_copy(arrived_hbm.at[at], arrived.at[at], sem.at[piece])
+
+    def push(piece):
+        at = pl.ds(piece * part, part)
+        return pltpu.make_async_copy(
+            image.at[:, at, :], image_hbm.at[:, at, :], sem.at[pieces + piece]
+        )
+
+    sums = pltpu.make_async_copy(sums_hbm, coupling_hbm, sem.at[2 * pieces])
+    for piece in range(pieces):
+        pull(piece).start()
+    sums.start()
+    for piece in range(pieces):
+        pull(piece).wait()
+
+        def unpack(step, carry):
+            tile = piece * (part // 8) + step
+            at = pl.ds(pl.multiple_of(tile * 8, 8), 8)
+            even = arrived[2 * tile]
+            odd = arrived[2 * tile + 1]
+            image[0, at, :] = jnp.where(low_half, even, pltpu.roll(odd, 4, 0))
+            image[1, at, :] = jnp.where(low_half, pltpu.roll(even, 4, 0), odd)
+            return carry
+
+        lax.fori_loop(0, part // 8, unpack, 0)
+        push(piece).start()
+    for piece in range(pieces):
+        push(piece).wait()
+    sums.wait()
 
 
 def solution(mesh):
@@ -555,22 +616,26 @@
         layers, width = direct.shape[2], direct.shape[3]
         offs = offsets.shape[0]
         f32, bf16 = jnp.float32, jnp.bfloat16
-        vmem = pl.BlockSpec(memory_space=pltpu.VMEM)
-        anywhere = pl.BlockSpec(memory_space=pl.ANY)
+        hbm = pl.BlockSpec(memory_space=pltpu.HBM)
         block = (orders, 8, width)
-        image, coupling = pl.pallas_call(
+        arrived, sums = pl.pallas_call(
             functools.partial(
                 kernel, orders, slabs, 1.0 / math.sqrt(layers * slabs * width)
             ),
             out_shape=(
-                jax.ShapeDtypeStruct((2, layers, width), f32),
+                jax.ShapeDtypeStruct(block, f32),
                 jax.ShapeDtypeStruct((2, offs), f32),
             ),
-            in_specs=[vmem, vmem, anywhere, anywhere, vmem, vmem, vmem, vmem]
-            + [pl.BlockSpec(memory_space=pltpu.SMEM)],
-            out_specs=(vmem, vmem),
+            in_specs=[hbm] * 9,
+            out_specs=(hbm, hbm),
             scratch_shapes=[
-                pltpu.VMEM(block, f32),
+                pltpu.VMEM((2, layers, width), f32),
+                pltpu.VMEM((2, layers, width), f32),
+                pltpu.VMEM((1, burner_temp.shape[0]), f32),
+                pltpu.VMEM((1, burner_gain.shape[0]), f32),
+                pltpu.VMEM((1, flame_cells.shape[0]), jnp.int32),
+                pltpu.VMEM((1, flame_weight.shape[0]), f32),
+                pltpu.SMEM((offs,), jnp.int32),
                 pltpu.VMEM(block, f32),
                 pltpu.VMEM(block, f32),
                 pltpu.VMEM(block, f32),
@@ -591,12 +656,13 @@
                 pltpu.VMEM((orders, 1, 128), f32),
                 pltpu.VMEM((orders, 1, 128), f32),
                 pltpu.VMEM((slabs, 1, 128), f32),
-                pltpu.SemaphoreType.DMA((2,)),
+                pltpu.VMEM((2, offs), f32),
+                pltpu.SemaphoreType.DMA((11,)),
                 pltpu.SemaphoreType.DMA((9,)),
                 pltpu.SemaphoreType.DMA((9,)),
             ],
             compiler_params=pltpu.CompilerParams(
-                collective_id=0, has_side_effects=True, vmem_limit_bytes=48 * 2**20
+                collective_id=0, has_side_effects=True, vmem_limit_bytes=58 * 2**20
             ),
         )(
             direct[0],
@@ -609,6 +675,21 @@
             flame_weight[None],
             offsets,
         )
+        image, coupling = pl.pallas_call(
+            write_out,
+            out_shape=(
+                jax.ShapeDtypeStruct((2, layers, width), f32),
+                jax.ShapeDtypeStruct((2, offs), f32),
+            ),
+            in_specs=[hbm, hbm],
+            out_specs=(hbm, hbm),
+            scratch_shapes=[
+                pltpu.VMEM(block, f32),
+                pltpu.VMEM((2, layers, width), f32),
+                pltpu.SemaphoreType.DMA((9,)),
+            ],
+            compiler_params=pltpu.CompilerParams(vmem_limit_bytes=58 * 2**20),
+        )(arrived, sums)
         return image[None], coupling[None]
 
     in_specs = (

time: 100 us -> 89.6 us (0.90)
  local copies, waits for them, and re-layouts: 8.42 us -> 0 us
  Pallas kernels: 90.2 us -> 88 us
    unnamed x18 -> x0, local copies, waits for them, and re-layouts: 8.42 us -> none
    pallas_call x1, Pallas kernels: 90.2 us -> 86 us  [local(): pl.pallas_call(functools.partial(kernel, orders, slabs, 1.0 / math.sqrt(l...]
    pallas_call x0 -> x1, Pallas kernels: none -> 2.02 us  [local(): pl.pallas_call(write_out, out_shape=(jax.ShapeDtypeStruct((2, layers, wid...]
where the time goes in v2:
time: 89.6 us; the launch traced here: 88.7 us
  Pallas kernels  88 us (98%)
    pallas_call x1, Pallas kernels, local(): pl.pallas_call(functools.partial(kernel, orders, slabs, 1.0 / math.sqrt(l...  86 us
    pallas_call x1, Pallas kernels, local(): pl.pallas_call(write_out, out_shape=(jax.ShapeDtypeStruct((2, layers, wid...  2.02 us

profile of v2, /device:TPU:1, one launch (start us, length us, event | category | flops | bytes accessed | tf_op | source)
XLA Modules:
  0.0 88.7 jit_solution(1732017817728763869)
XLA Ops:
  0.6 86.0 %shard_map.104 = (f32[32,8,1024]{2,1,0:T(8,128)}, f32[2,4]{1,0:T(2,128)}) custom-call(f32[2,128,1024]{2,1,0:T(8,128)} %bitcast.8, f32[2,128,1024]{2,1,0:T(8,128)} %bitcast.9, f32[128,1024]{1,0:T(8,128)} %sound_hbm.1, f32[1024,1024]{1,0:T(8,128)} %transverse_hbm.1, f32[1,32]{1,0:T(1,128)} %bitcast.12, f32[1,32]{1,0:T(1,128)} %bitcast.13, s32[1,4096]{1,0:T(1,128)} %bitcast.10, ...), custom_call_target="tpu_custom_call" | custom-call | tf_op jit(solution)/shard_map/pallas_call | solution.py:621
  86.6 2.0 %shard_map.105 = (f32[2,128,1024]{2,1,0:T(8,128)}, f32[2,4]{1,0:T(2,128)}) custom-call(f32[32,8,1024]{2,1,0:T(8,128)} %get-tuple-element.6.arrived_hbm, f32[2,4]{1,0:T(2,128)} %get-tuple-element.7.sums_hbm), custom_call_target="tpu_custom_call" | custom-call | tf_op jit(solution)/shard_map/pallas_call | solution.py:678

commit v3 on v2

--- a/solution.py
+++ b/solution.py
@@ -11,8 +11,8 @@
 MESH = pl.DeviceIdType.MESH
 STRIDE = 11
 EARLY = 20
-FIRST = 24
-SECOND = 30
+MIDDLE = 26
+FIRST = 20
 
 
 def kernel(
@@ -52,6 +52,7 @@
     sound_pad,
     halo_send,
     halo_recv,
+    halo_relay,
     turn_cos,
     turn_sin,
     csend,
@@ -112,16 +113,43 @@
         "order": lax.rem(me + 1, orders),
         "slab": lax.rem(slab + lax.div(me + 1, orders), slabs),
     }
+    place_in_plane = lax.rem(me, 4)
+    crosses_up = jnp.logical_and(place_in_plane == 0, has_above)
+    crosses_down = jnp.logical_and(place_in_plane == 3, has_below)
+    within_up = jnp.logical_and(place_in_plane != 0, has_above)
+    within_down = jnp.logical_and(place_in_plane != 3, has_below)
+    relays_up = jnp.logical_and(
+        place_in_plane == 2, jnp.logical_or(me > 3, slab > 0)
+    )
+    relays_down = jnp.logical_and(
+        place_in_plane == 1, jnp.logical_or(me < orders - 4, slab < slabs - 1)
+    )
+    far_up_dev = {
+        "order": lax.rem(me + orders - 3, orders),
+        "slab": lax.rem(slab + slabs - lax.div(orders + 2 - me, orders), slabs),
+    }
+    far_down_dev = {
+        "order": lax.rem(me + 3, orders),
+        "slab": lax.rem(slab + lax.div(me + 3, orders), slabs),
+    }
+    greet_up_dev = {"order": orders - 3, "slab": lax.rem(slab + slabs - 1, slabs)}
+    greet_down_dev = {"order": 2, "slab": lax.rem(slab + 1, slabs)}
     lax.fori_loop(1, orders, greet_order, 0)
     lax.fori_loop(1, slabs, greet_slab, 0)
 
     @pl.when(has_above_slab)
     def _():
         pl.semaphore_signal(barrier, inc=1, device_id=above_dev, device_id_type=MESH)
+        pl.semaphore_signal(
+            barrier, inc=1, device_id=greet_up_dev, device_id_type=MESH
+        )
 
     @pl.when(has_below_slab)
     def _():
         pl.semaphore_signal(barrier, inc=1, device_id=below_dev, device_id_type=MESH)
+        pl.semaphore_signal(
+            barrier, inc=1, device_id=greet_down_dev, device_id_type=MESH
+        )
 
     sub = lax.broadcasted_iota(jnp.int32, (8, 128), 0)
     lane = lax.broadcasted_iota(jnp.int32, (8, 128), 1)
@@ -151,7 +179,10 @@
     fetch_d.wait()
     pack(direct_ref, dstage)
 
+    near_top = jnp.logical_and(me == 2, slab > 0)
+    near_bottom = jnp.logical_and(me == orders - 3, slab < slabs - 1)
     extra = has_above_slab.astype(jnp.int32) + has_below_slab.astype(jnp.int32)
+    extra = extra + near_top.astype(jnp.int32) + near_bottom.astype(jnp.int32)
     pl.semaphore_wait(barrier, orders - 1 + slabs - 1 + extra)
 
     def scatter_copy(stage, into, sem, step):
@@ -346,35 +377,67 @@
 
     lax.fori_loop(0, orders // 4, edges, 0)
 
-    def halo_up():
+    near, rest = pl.ds(0, orders), pl.ds(orders, orders)
+
+    def halo(source, into, sem, recv, to):
         return pltpu.make_async_remote_copy(
-            src_ref=halo_send.at[0],
-            dst_ref=halo_recv.at[1],
-            send_sem=send_sem.at[5],
-            recv_sem=recv_sem.at[5],
-            device_id=above_dev,
+            src_ref=source,
+            dst_ref=into,
+            send_sem=send_sem.at[sem],
+            recv_sem=recv_sem.at[recv],
+            device_id=to,
             device_id_type=MESH,
         )
 
-    def halo_down():
-        return pltpu.make_async_remote_copy(
-            src_ref=halo_send.at[1],
-            dst_ref=halo_recv.at[0],
-            send_sem=send_sem.at[6],
-            recv_sem=recv_sem.at[6],
-            device_id=below_dev,
-            device_id_type=MESH,
-        )
+    def up_near():
+        return halo(halo_send.at[0, near], halo_recv.at[1, near], 5, 5, above_dev)
+
+    def up_rest():
+        return halo(halo_send.at[0, rest], halo_recv.at[1, rest], 9, 9, above_dev)
+
+    def up_relay():
+        return halo(halo_send.at[0, rest], halo_relay, 9, 11, order_dev(lax.rem(me + 2, orders)))
+
+    def up_far():
+        return halo(halo_relay, halo_recv.at[1, rest], 11, 9, far_up_dev)
+
+    def down_near():
+        return halo(halo_send.at[1, near], halo_recv.at[0, near], 6, 6, below_dev)
+
+    def down_rest():
+        return halo(halo_send.at[1, rest], halo_recv.at[0, rest], 10, 10, below_dev)
+
+    def down_relay():
+        return halo(halo_send.at[1, rest], halo_relay, 10, 11, order_dev(lax.rem(me + orders - 2, orders)))
+
+    def down_far():
+        return halo(halo_relay, halo_recv.at[0, rest], 11, 10, far_down_dev)
+
+    @pl.when(crosses_up)
+    def _():
+        up_relay().start()
+
+    @pl.when(crosses_down)
+    def _():
+        down_relay().start()
 
     @pl.when(has_above)
     def _():
-        halo_up().start()
+        up_near().start()
 
     @pl.when(has_below)
     def _():
-        halo_down().start()
-
-    scatter(astage, adj, 1, EARLY, orders)
+        down_near().start()
+
+    @pl.when(within_up)
+    def _():
+        up_rest().start()
+
+    @pl.when(within_down)
+    def _():
+        down_rest().start()
+
+    scatter(astage, adj, 1, EARLY, MIDDLE)
 
     def split(group, carry):
         value = field[pl.ds(4 * group, 4)].reshape(32, width)
@@ -385,6 +448,18 @@
         return carry
 
     lax.fori_loop(0, orders // 4, split, 0)
+
+    @pl.when(relays_up)
+    def _():
+        up_relay().wait_recv()
+        up_far().start()
+
+    @pl.when(relays_down)
+    def _():
+        down_relay().wait_recv()
+        down_far().start()
+
+    scatter(astage, adj, 1, MIDDLE, orders)
 
     def across(block, carry):
         at = pl.ds(pl.multiple_of(block * 256, 256), 256)
@@ -400,13 +475,13 @@
 
     @pl.when(has_below)
     def _():
-        halo_up_recv = halo_up()
-        halo_up_recv.wait_recv()
+        up_near().wait_recv()
+        up_rest().wait_recv()
 
     @pl.when(has_above)
     def _():
-        halo_down_recv = halo_down()
-        halo_down_recv.wait_recv()
+        down_near().wait_recv()
+        down_rest().wait_recv()
 
     @pl.when(jnp.logical_not(has_below))
     def _():
@@ -511,7 +586,7 @@
     lax.fori_loop(0, orders, couple, 0)
     scatter(csend, cpart, 7, 1, orders)
     cpart[me] = csend[me]
-    lax.fori_loop(FIRST, SECOND, give, 0)
+    lax.fori_loop(FIRST, orders, give, 0)
     wait_bytes(others(cpart), recv_sem.at[7])
     total = cpart[0]
     for k in range(1, orders):
@@ -534,7 +609,6 @@
 
     lax.fori_loop(1, slabs, slab_start, 0)
 
-    lax.fori_loop(SECOND, orders, give, 0)
     istage[me] = mixed(me)
     keep = pltpu.make_async_copy(istage.at[me], arrived.at[me], local_sem.at[9])
     keep.start()
@@ -559,11 +633,21 @@
 
     @pl.when(has_above)
     def _():
-        halo_up().wait_send()
+        up_near().wait_send()
+        up_rest().wait_send()
 
     @pl.when(has_below)
     def _():
-        halo_down().wait_send()
+        down_near().wait_send()
+        down_rest().wait_send()
+
+    @pl.when(relays_up)
+    def _():
+        up_far().wait_send()
+
+    @pl.when(relays_down)
+    def _():
+        down_far().wait_send()
 
 
 def write_out(arrived_hbm, sums_hbm, image_hbm, coupling_hbm, arrived, image, sem):
@@ -651,6 +735,7 @@
                 pltpu.VMEM((layers + 16, width), f32),
                 pltpu.VMEM((2, 2 * orders, width), f32),
                 pltpu.VMEM((2, 2 * orders, width), f32),
+                pltpu.VMEM((orders, width), f32),
                 pltpu.VMEM((orders, 8, 128), f32),
                 pltpu.VMEM((orders, 8, 128), f32),
                 pltpu.VMEM((orders, 1, 128), f32),
@@ -658,8 +743,8 @@
                 pltpu.VMEM((slabs, 1, 128), f32),
                 pltpu.VMEM((2, offs), f32),
                 pltpu.SemaphoreType.DMA((11,)),
-                pltpu.SemaphoreType.DMA((9,)),
-                pltpu.SemaphoreType.DMA((9,)),
+                pltpu.SemaphoreType.DMA((12,)),
+                pltpu.SemaphoreType.DMA((12,)),
             ],
             compiler_params=pltpu.CompilerParams(
                 collective_id=0, has_side_effects=True, vmem_limit_bytes=58 * 2**20

time: 89.6 us -> 86.9 us (0.970)
  Pallas kernels: 88 us -> 86.2 us
    pallas_call x1, Pallas kernels: 86 us -> 84.2 us  [local(): pl.pallas_call(functools.partial(kernel, orders, slabs, 1.0 / math.sqrt(l...]
where the time goes in v3:
time: 86.9 us; the launch traced here: 86.8 us
  Pallas kernels  86.2 us (99%)
    pallas_call x1, Pallas kernels, local(): pl.pallas_call(functools.partial(kernel, orders, slabs, 1.0 / math.sqrt(l...  84.2 us
    pallas_call x1, Pallas kernels, local(): pl.pallas_call(write_out, out_shape=(jax.ShapeDtypeStruct((2, layers, wid...  2.02 us

profile of v3, /device:TPU:1, one launch (start us, length us, event | category | flops | bytes accessed | tf_op | source)
XLA Modules:
  0.0 86.8 jit_solution(5969694740034958427)
XLA Ops:
  0.6 84.2 %shard_map.104 = (f32[32,8,1024]{2,1,0:T(8,128)}, f32[2,4]{1,0:T(2,128)}) custom-call(f32[2,128,1024]{2,1,0:T(8,128)} %bitcast.8, f32[2,128,1024]{2,1,0:T(8,128)} %bitcast.9, f32[128,1024]{1,0:T(8,128)} %sound_hbm.1, f32[1024,1024]{1,0:T(8,128)} %transverse_hbm.1, f32[1,32]{1,0:T(1,128)} %bitcast.12, f32[1,32]{1,0:T(1,128)} %bitcast.13, s32[1,4096]{1,0:T(1,128)} %bitcast.10, ...), custom_call_target="tpu_custom_call" | custom-call | tf_op jit(solution)/shard_map/pallas_call | solution.py:705
  84.8 2.0 %shard_map.105 = (f32[2,128,1024]{2,1,0:T(8,128)}, f32[2,4]{1,0:T(2,128)}) custom-call(f32[32,8,1024]{2,1,0:T(8,128)} %get-tuple-element.6.arrived_hbm, f32[2,4]{1,0:T(2,128)} %get-tuple-element.7.sums_hbm), custom_call_target="tpu_custom_call" | custom-call | tf_op jit(solution)/shard_map/pallas_call | solution.py:763

commit v4 on v3

--- a/solution.py
+++ b/solution.py
@@ -10,9 +10,10 @@
 
 MESH = pl.DeviceIdType.MESH
 STRIDE = 11
+IMAGE_STRIDE = 5
 EARLY = 20
 MIDDLE = 26
-FIRST = 20
+FIRST = 18
 
 
 def kernel(
@@ -74,8 +75,8 @@
     def order_dev(which):
         return {"order": which}
 
-    def peer(step):
-        return lax.rem(me + lax.rem(step * STRIDE, orders), orders)
+    def peer(step, stride=STRIDE):
+        return lax.rem(me + lax.rem(step * stride, orders), orders)
 
     def fetch(source, into, sem):
         copy = pltpu.make_async_copy(source, into, local_sem.at[sem])
@@ -186,7 +187,7 @@
     pl.semaphore_wait(barrier, orders - 1 + slabs - 1 + extra)
 
     def scatter_copy(stage, into, sem, step):
-        to = peer(step)
+        to = peer(step, STRIDE if sem < 2 else IMAGE_STRIDE)
         return pltpu.make_async_remote_copy(
             src_ref=stage.at[to],
             dst_ref=into.at[me],
@@ -537,7 +538,7 @@
         return plain + sign_w * pltpu.roll(turned, 4, 0)
 
     def give(step, carry):
-        target = peer(step)
+        target = peer(step, IMAGE_STRIDE)
         istage[target] = mixed(target)
         scatter_copy(istage, arrived, 2, step).start()
         return carry

time: 86.9 us -> 85.3 us (0.982)
  Pallas kernels: 86.2 us -> 84.5 us
    pallas_call x1, Pallas kernels: 84.2 us -> 82.5 us  [local(): pl.pallas_call(functools.partial(kernel, orders, slabs, 1.0 / math.sqrt(l...]
where the time goes in v4:
time: 85.3 us; the launch traced here: 85.2 us
  Pallas kernels  84.5 us (99%)
    pallas_call x1, Pallas kernels, local(): pl.pallas_call(functools.partial(kernel, orders, slabs, 1.0 / math.sqrt(l...  82.5 us
    pallas_call x1, Pallas kernels, local(): pl.pallas_call(write_out, out_shape=(jax.ShapeDtypeStruct((2, layers, wid...  2.02 us

profile of v4, /device:TPU:1, one launch (start us, length us, event | category | flops | bytes accessed | tf_op | source)
XLA Modules:
  0.0 85.2 jit_solution(5791223912176626827)
XLA Ops:
  0.6 82.5 %shard_map.104 = (f32[32,8,1024]{2,1,0:T(8,128)}, f32[2,4]{1,0:T(2,128)}) custom-call(f32[2,128,1024]{2,1,0:T(8,128)} %bitcast.8, f32[2,128,1024]{2,1,0:T(8,128)} %bitcast.9, f32[128,1024]{1,0:T(8,128)} %sound_hbm.1, f32[1024,1024]{1,0:T(8,128)} %transverse_hbm.1, f32[1,32]{1,0:T(1,128)} %bitcast.12, f32[1,32]{1,0:T(1,128)} %bitcast.13, s32[1,4096]{1,0:T(1,128)} %bitcast.10, ...), custom_call_target="tpu_custom_call" | custom-call | tf_op jit(solution)/shard_map/pallas_call | solution.py:706
  83.1 2.0 %shard_map.105 = (f32[2,128,1024]{2,1,0:T(8,128)}, f32[2,4]{1,0:T(2,128)}) custom-call(f32[32,8,1024]{2,1,0:T(8,128)} %get-tuple-element.6.arrived_hbm, f32[2,4]{1,0:T(2,128)} %get-tuple-element.7.sums_hbm), custom_call_target="tpu_custom_call" | custom-call | tf_op jit(solution)/shard_map/pallas_call | solution.py:764

commit v5 on v4

--- a/solution.py
+++ b/solution.py
@@ -83,7 +83,16 @@
         copy.start()
         return copy
 
-    fetch_d = fetch(direct_hbm, direct_ref, 2)
+    pieces = 4
+    part = layers // pieces
+    fetch_d = [
+        fetch(
+            direct_hbm.at[:, pl.ds(piece * part, part), :],
+            direct_ref.at[:, pl.ds(piece * part, part), :],
+            11 + piece,
+        )
+        for piece in range(pieces)
+    ]
 
     barrier = pltpu.get_barrier_semaphore()
 
@@ -156,7 +165,7 @@
     lane = lax.broadcasted_iota(jnp.int32, (8, 128), 1)
     sub_w = lax.broadcasted_iota(jnp.int32, (8, width), 0)
 
-    def pack(source, stage):
+    def pack(source, stage, first, end):
         def body(tile, carry):
             at = pl.multiple_of(tile * 8, 8)
             re = source[0, pl.ds(at, 8), :]
@@ -165,7 +174,7 @@
             stage[2 * tile + 1] = jnp.where(sub_w < 4, pltpu.roll(re, 4, 0), im)
             return carry
 
-        lax.fori_loop(0, layers // 8, body, 0)
+        lax.fori_loop(first, end, body, 0)
 
     fetch_c = fetch(sound_hbm, sound_pad.at[pl.ds(8, layers)], 1)
     fetch_a = fetch(adjoint_hbm, adjoint_ref, 3)
@@ -177,8 +186,9 @@
         fetch(weight_hbm, weight_ref, 8),
     ]
     fetch_t = fetch(transverse_hbm, tmat, 0)
-    fetch_d.wait()
-    pack(direct_ref, dstage)
+    for piece in range(pieces):
+        fetch_d[piece].wait()
+        pack(direct_ref, dstage, piece * part // 8, (piece + 1) * part // 8)
 
     near_top = jnp.logical_and(me == 2, slab > 0)
     near_bottom = jnp.logical_and(me == orders - 3, slab < slabs - 1)
@@ -244,7 +254,7 @@
         sound_down().start()
 
     fetch_a.wait()
-    pack(adjoint_ref, astage)
+    pack(adjoint_ref, astage, 0, layers // 8)
     scatter(astage, adj, 1, 1, EARLY)
     adj[me] = astage[me]
 
@@ -743,7 +753,7 @@
                 pltpu.VMEM((orders, 1, 128), f32),
                 pltpu.VMEM((slabs, 1, 128), f32),
                 pltpu.VMEM((2, offs), f32),
-                pltpu.SemaphoreType.DMA((11,)),
+                pltpu.SemaphoreType.DMA((15,)),
                 pltpu.SemaphoreType.DMA((12,)),
                 pltpu.SemaphoreType.DMA((12,)),
             ],

time: 85.3 us -> 85.3 us (level)
  no operation moved by 1% of the time
where the time goes in v5:
time: 85.3 us; the launch traced here: 85.2 us
  Pallas kernels  84.6 us (99%)
    pallas_call x1, Pallas kernels, local(): pl.pallas_call(functools.partial(kernel, orders, slabs, 1.0 / math.sqrt(l...  82.5 us
    pallas_call x1, Pallas kernels, local(): pl.pallas_call(write_out, out_shape=(jax.ShapeDtypeStruct((2, layers, wid...  2.02 us

profile of v5, /device:TPU:1, one launch (start us, length us, event | category | flops | bytes accessed | tf_op | source)
XLA Modules:
  0.0 85.2 jit_solution(10894655348664130808)
XLA Ops:
  0.6 82.5 %shard_map.104 = (f32[32,8,1024]{2,1,0:T(8,128)}, f32[2,4]{1,0:T(2,128)}) custom-call(f32[2,128,1024]{2,1,0:T(8,128)} %bitcast.8, f32[2,128,1024]{2,1,0:T(8,128)} %bitcast.9, f32[128,1024]{1,0:T(8,128)} %sound_hbm.1, f32[1024,1024]{1,0:T(8,128)} %transverse_hbm.1, f32[1,32]{1,0:T(1,128)} %bitcast.12, f32[1,32]{1,0:T(1,128)} %bitcast.13, s32[1,4096]{1,0:T(1,128)} %bitcast.10, ...), custom_call_target="tpu_custom_call" | custom-call | tf_op jit(solution)/shard_map/pallas_call | solution.py:716
  83.2 2.0 %shard_map.105 = (f32[2,128,1024]{2,1,0:T(8,128)}, f32[2,4]{1,0:T(2,128)}) custom-call(f32[32,8,1024]{2,1,0:T(8,128)} %get-tuple-element.6.arrived_hbm, f32[2,4]{1,0:T(2,128)} %get-tuple-element.7.sums_hbm), custom_call_target="tpu_custom_call" | custom-call | tf_op jit(solution)/shard_map/pallas_call | solution.py:774
